TPU v7x, 32 devices: a whole 2x2x4 slice. The times are simulated.
32 devices in a mesh: pass: 8 (over y, x, core), kv: 4 (over z).
Axes of the slice: x: 2, y: 2, z: 4, core: 2. Of those that a mesh axis runs over, the one named last changes fastest.
Arguments:
- queries: bfloat16 [8, 64, 4096], P('pass', None, 'kv'), may hold values from -40 to 40
- suffix_keys: bfloat16 [8, 64, 512], P('pass', None, 'kv'), may hold values from -5 to 5
- suffix_values: bfloat16 [8, 64, 512], P('pass', None, 'kv'), may hold values from -40 to 40
- passage_keys: bfloat16 [32, 1024, 512], P('pass', None, 'kv'), may hold values from -5 to 5
- passage_values: bfloat16 [32, 1024, 512], P('pass', None, 'kv'), may hold values from -40 to 40
- fresh_keys: bfloat16 [8, 8, 128, 512], P('pass', None, None, 'kv'), may hold values from -5 to 5
- fresh_values: bfloat16 [8, 8, 128, 512], P('pass', None, None, 'kv'), may hold values from -40 to 40
- citations: int32 [8, 8], P('pass'), may hold values from 0 to 31, all different within a row; in each aligned block of 8 rows (0 to 7, 8 to 15, ...) at most 4 rows name the same one
- selected: int32 [8, 8, 128], P('pass'), may hold values from 0 to 1023, as said below
Outputs:
- attention: bfloat16 [8, 64, 4096], P('pass', 'kv')
Inputs may be any that keep to these rules, and one draw needn't show every extreme that they name: `citations`: each request cites 8 distinct passages; every passage is cited; no passage is cited by more than 4 requests, a bound that some block reaches. `selected`: each list holds 128 distinct positions of its passage.
All inputs are finite; a program needn't handle non-finite values.
Results may differ from a plain program's by a relative error of at most 0.0053.
Values may be sent and summed in bfloat16 or wider, within the bound.
A program may use at most 128 MiB of HBM per device.

v0:
```python
import functools
import math

import jax
import jax.numpy as jnp
from jax import lax
from jax.experimental import pallas as pl
from jax.experimental.pallas import tpu as pltpu
from jax.sharding import PartitionSpec as P

HD = 128
MESH = pl.DeviceIdType.MESH
very_low = -1e30
FACTOR = math.log2(math.e) / math.sqrt(HD)
ONES = 16
CHUNK = 256


def nt_dot(a, b):
    return lax.dot_general(a, b, (((1,), (1,)), ((), ())), preferred_element_type=jnp.float32)


def nn_dot(a, b):
    return jnp.dot(a, b, preferred_element_type=jnp.float32)


def stack_heads(rows, group_size):
    return jnp.concatenate([rows[:, g * HD : (g + 1) * HD] for g in range(group_size)], axis=0)


def gather_kernel(
    n,
    q_ref,
    sk_ref,
    sv_ref,
    fk_ref,
    fv_ref,
    cite_ref,
    sel_ref,
    q_all,
    cite_all,
    sel_all,
    host_acc,
    host_max,
    cite_buf,
    cite_in,
    q_buf,
    sk_buf,
    sv_buf,
    fk_buf,
    fv_buf,
    in_sem,
    own_sem,
    send_sem,
    recv_sem,
    fsend_sem,
    frecv_sem,
):
    loads = [pltpu.make_async_copy(cite_ref, cite_in, in_sem.at[5])]
    for i, (source, place) in enumerate(
        ((q_ref, q_buf), (sk_ref, sk_buf), (fk_ref, fk_buf), (fv_ref, fv_buf), (sv_ref, sv_buf))
    ):
        loads.append(pltpu.make_async_copy(source, place, in_sem.at[i]))
    for copy in loads:
        copy.start()
    me = lax.axis_index("pass")
    chip, core = me // 2, me % 2
    chips = n // 2
    sibling = chip * 2 + (1 - core)

    def peer(off):
        return ((chip + off) % chips) * 2 + core

    def origin(off, lane):
        return ((chip + chips - off) % chips) * 2 + lane

    barrier = pltpu.get_barrier_semaphore()
    for target in [sibling] + [peer(off) for off in range(1, chips)]:
        pl.semaphore_signal(barrier, inc=1, device_id={"pass": target}, device_id_type=MESH)
    cite_buf[...] = jnp.zeros_like(cite_buf)
    loads[0].wait()
    cite_buf[0:1, 0 : cite_ref.shape[1]] = cite_in[...]
    pl.semaphore_wait(barrier, chips)

    sources = (q_ref.at[0], cite_buf, sel_ref.at[0])
    places = (q_all, cite_all, sel_all)

    def remote(i, off, source, slot, target, send, recv):
        return pltpu.make_async_remote_copy(
            src_ref=source,
            dst_ref=places[i].at[slot],
            send_sem=send.at[i, off],
            recv_sem=recv.at[i, off],
            device_id={"pass": target},
            device_id_type=MESH,
        )

    sends = []
    for off in list(range(1, chips)) + [0]:
        for i in (1, 2, 0):
            if off == 0:
                copy = remote(i, 0, sources[i], me, sibling, fsend_sem, frecv_sem)
            else:
                copy = remote(i, off, sources[i], me, peer(off), send_sem, recv_sem)
            copy.start()
            sends.append(copy)
    own = []
    for i in range(3):
        copy = pltpu.make_async_copy(sources[i], places[i].at[me], own_sem.at[i])
        copy.start()
        own.append(copy)

    for copy in loads[1:]:
        copy.wait()
    tokens = q_ref.shape[1]
    group_size = q_ref.shape[2] // HD
    rows = tokens * group_size
    q = stack_heads(q_buf[0], group_size)
    fresh = fk_ref.shape[1] * fk_ref.shape[2]
    fk = fk_buf[0].reshape(fresh, HD)
    fv_t = fv_buf[0].reshape(fresh, HD).T
    fv_t = jnp.concatenate([fv_t, jnp.ones((ONES, fresh), jnp.bfloat16)], axis=0)
    sv_t = sv_buf[0].astype(jnp.float32).T.astype(jnp.bfloat16)
    sv_t = jnp.concatenate([sv_t, jnp.ones((ONES, tokens), jnp.bfloat16)], axis=0)
    for lo in range(0, rows, CHUNK):
        block = q[lo : lo + CHUNK]
        fs = nt_dot(fk, block)
        ss = nt_dot(sk_buf[0], block)
        key_at = lax.broadcasted_iota(jnp.int32, (tokens, CHUNK), 0)
        token_at = (lax.broadcasted_iota(jnp.int32, (tokens, CHUNK), 1) + lo) % tokens
        ss = jnp.where(key_at <= token_at, ss, very_low)
        top = jnp.maximum(
            jnp.max(fs, axis=0, keepdims=True), jnp.max(ss, axis=0, keepdims=True)
        )
        fw = jnp.exp2((fs - top) * FACTOR).astype(jnp.bfloat16)
        sw = jnp.exp2((ss - top) * FACTOR).astype(jnp.bfloat16)
        host_acc[:, lo : lo + CHUNK] = nn_dot(fv_t, fw) + nn_dot(sv_t, sw)
        host_max[:, lo : lo + CHUNK] = jnp.broadcast_to(top, (8, CHUNK))

    for off in range(1, chips):
        slot = origin(off, core)
        for i in (1, 2, 0):
            remote(i, off, sources[i], slot, peer(off), send_sem, recv_sem).wait_recv()
            copy = remote(i, off, places[i].at[slot], slot, sibling, fsend_sem, frecv_sem)
            copy.start()
            sends.append(copy)
    for off in range(chips):
        slot = origin(off, 1 - core)
        for i in range(3):
            remote(i, off, sources[i], slot, sibling, fsend_sem, frecv_sem).wait_recv()
    for copy in own:
        copy.wait()
    for copy in sends:
        copy.wait_send()


def slot_kernel(
    cites,
    q_hbm,
    sel_hbm,
    k_hbm,
    v_hbm,
    out_ref,
    stat_ref,
    q_all,
    sel_all,
    k_ref,
    v_ref,
    v_t,
    acc,
    top,
    peak,
    bias,
    first,
    second,
    live,
    in_sem,
):
    me = lax.axis_index("pass")
    total, tokens, width = q_all.shape
    group_size = width // HD
    rows = tokens * group_size
    half = rows // 2
    heads_half = group_size // 2
    local, length, _ = k_ref.shape
    cite_count = sel_all.shape[1]
    picks = sel_all.shape[2]
    loads = []
    for i, (source, place) in enumerate(
        ((v_hbm, v_ref), (sel_hbm, sel_all), (k_hbm, k_ref), (q_hbm, q_all))
    ):
        copy = pltpu.make_async_copy(source, place, in_sem.at[i])
        copy.start()
        loads.append(copy)

    def collect(i, count):
        live[count] = i
        cited = cites[i // cite_count, 0, i % cite_count]
        return count + (cited // local == me).astype(jnp.int32)

    count = lax.fori_loop(0, total * cite_count, collect, 0)
    acc[...] = jnp.zeros_like(acc)
    top[...] = jnp.full_like(top, very_low)
    loads[0].wait()
    for p in range(local):
        v_t[p, 0:HD, :] = v_ref[p].T
        v_t[p, HD:, :] = jnp.ones((ONES, length), jnp.bfloat16)
    for copy in loads[1:]:
        copy.wait()

    def where(i):
        at = live[jnp.minimum(i, jnp.maximum(count - 1, 0))]
        r, c = at // cite_count, at % cite_count
        return r, c, cites[r, 0, c] % local

    def fill_bias(r, c):
        at = lax.broadcasted_iota(jnp.int32, (length, picks), 0)
        picked = sel_all[r, pl.ds(c, 1), :]
        bias[...] = jnp.where(at == picked, very_low, 0.0).astype(jnp.bfloat16)

    def score(r, p, side, place):
        keys = jnp.concatenate([k_ref[p], bias[...]], axis=1)
        cut = heads_half * HD
        q = stack_heads(q_all[r, :, side * cut : (side + 1) * cut], heads_half)
        q = jnp.concatenate([q, jnp.ones((half, picks), jnp.bfloat16)], axis=1)
        s = nt_dot(keys, q)
        place[...] = s
        peak[side] = jnp.broadcast_to(jnp.max(s, axis=0, keepdims=True), (8, half))

    def weigh(r, p, side, place):
        lo, hi = side * half, (side + 1) * half
        old = top[r, 0:1, lo:hi]
        new = jnp.maximum(old, peak[side, 0:1, :])
        w = jnp.exp2((place[...] - new) * FACTOR).astype(jnp.bfloat16)
        scale = jnp.exp2((old - new) * FACTOR)
        acc[r, :, lo:hi] = acc[r, :, lo:hi] * scale + nn_dot(v_t[p], w)
        top[r, :, lo:hi] = jnp.broadcast_to(new, (8, half))

    r, c, p = where(0)
    fill_bias(r, c)
    score(r, p, 0, first)

    def one_slot(i, carry):
        r, c, p = where(i)
        score(r, p, 1, second)
        weigh(r, p, 0, first)
        r_next, c_next, p_next = where(i + 1)
        fill_bias(r_next, c_next)
        score(r_next, p_next, 0, first)
        weigh(r, p, 1, second)
        return carry

    lax.fori_loop(0, count, one_slot, 0)

    def finish(r, carry):
        weight = acc[r, HD : HD + 8, :]
        out = acc[r, 0:HD, :] * (1.0 / jnp.maximum(weight[0:1], 1.0))
        upper = lax.broadcasted_iota(jnp.int32, weight.shape, 0) < 4
        stat = jnp.where(upper, top[r], weight)
        for side in range(2):
            lo, hi = side * half, (side + 1) * half
            out_ref[r, side] = out[:, lo:hi].astype(jnp.bfloat16)
            stat_ref[r, side] = stat[:, lo:hi]
        return carry

    lax.fori_loop(0, total, finish, 0)


def merge_kernel(
    n,
    kv,
    out_all,
    stat_all,
    host_acc_hbm,
    host_max_hbm,
    result,
    host_acc,
    host_max,
    mine_out,
    mine_stat,
    pair_out,
    pair_stat,
    send_out,
    send_stat,
    got_out,
    got_stat,
    kv_send,
    kv_recv,
    host_sem,
    own_sem,
    pair_send_sem,
    pair_recv_sem,
    send_sem,
    recv_sem,
    kv_send_sem,
    kv_recv_sem,
):
    me = lax.axis_index("pass")
    my_kv = lax.axis_index("kv")
    chip, core = me // 2, me % 2
    chips = n // 2
    sibling = chip * 2 + (1 - core)
    pieces = out_all.shape[1]
    part, width = kv_send.shape[2:]
    heads = width // HD
    tokens = part * kv

    def target_chip(off):
        return (chip + off) % chips

    def source_chip(off):
        return (chip + chips - off) % chips

    barrier = pltpu.get_barrier_semaphore()
    for other in [sibling] + [target_chip(off) * 2 + core for off in range(1, chips)]:
        pl.semaphore_signal(barrier, inc=1, device_id={"pass": other}, device_id_type=MESH)
    for off in range(1, kv):
        pl.semaphore_signal(
            barrier, inc=1, device_id={"kv": (my_kv + off) % kv}, device_id_type=MESH
        )
    order = list(range(1, chips)) + [0]
    tables = ((out_all, mine_out, pair_out), (stat_all, mine_stat, pair_stat))
    own = {}
    for h in range(pieces):
        for off in order:
            for i, (source, place, _) in enumerate(tables):
                t = target_chip(off)
                own[h, off, i] = pltpu.make_async_copy(
                    source.at[t * 2 + core, h], place.at[off, h], own_sem.at[i, h, off]
                )
                own[h, off, i].start()
    loads = [
        pltpu.make_async_copy(host_acc_hbm, host_acc, host_sem.at[0]),
        pltpu.make_async_copy(host_max_hbm, host_max, host_sem.at[1]),
    ]
    for copy in loads:
        copy.start()
    pl.semaphore_wait(barrier, chips + kv - 1)

    def to_sibling(i, h, off):
        source, _, place = tables[i]
        return pltpu.make_async_remote_copy(
            src_ref=source.at[target_chip(off) * 2 + 1 - core, h],
            dst_ref=place.at[off, h],
            send_sem=pair_send_sem.at[i, h, off],
            recv_sem=pair_recv_sem.at[i, h, off],
            device_id={"pass": sibling},
            device_id_type=MESH,
        )

    def to_chip(i, h, off):
        source, place = ((send_out, got_out), (send_stat, got_stat))[i]
        return pltpu.make_async_remote_copy(
            src_ref=source.at[off, h],
            dst_ref=place.at[off, h],
            send_sem=send_sem.at[i, h, off],
            recv_sem=recv_sem.at[i, h, off],
            device_id={"pass": target_chip(off) * 2 + core},
            device_id_type=MESH,
        )

    def across(h, off, target, slot):
        return pltpu.make_async_remote_copy(
            src_ref=kv_send.at[h, target],
            dst_ref=kv_recv.at[h, slot],
            send_sem=kv_send_sem.at[h, off],
            recv_sem=kv_recv_sem.at[h, off],
            device_id={"kv": target},
            device_id_type=MESH,
        )

    sends = []
    for h in range(pieces):
        for off in order:
            for i in (1, 0):
                copy = to_sibling(i, h, off)
                copy.start()
                sends.append(copy)

    def pair_ready(h, off):
        for i in range(2):
            own[h, off, i].wait()
            to_sibling(i, h, off).wait_recv()

    def weighted(outs, stats):
        ceiling = stats[0][0]
        for top, _ in stats[1:]:
            ceiling = jnp.maximum(ceiling, top)
        numer, denom = 0.0, 0.0
        for out, (top, weight) in zip(outs, stats):
            scale = jnp.exp2((top - ceiling) * FACTOR)
            if weight is None:
                out, weight = out[0:HD], out[HD : HD + 1]
                numer = numer + out * scale
                denom = denom + weight * scale
            else:
                share = weight * scale
                numer = numer + out.astype(jnp.float32) * share
                denom = denom + share
        return ceiling, numer, denom

    def stats_of(ref, off, h):
        return ref[off, h, 0:1, :], ref[off, h, 4:5, :]

    for h in range(pieces):
        for off in range(1, chips):
            pair_ready(h, off)
            top, numer, denom = weighted(
                [mine_out[off, h], pair_out[off, h]],
                [stats_of(mine_stat, off, h), stats_of(pair_stat, off, h)],
            )
            send_out[off, h] = (numer / jnp.maximum(denom, 1.0)).astype(jnp.bfloat16)
            send_stat[off, h] = jnp.concatenate(
                [jnp.broadcast_to(top, (4, top.shape[1])), jnp.broadcast_to(denom, (4, top.shape[1]))]
            )
            for i in (1, 0):
                copy = to_chip(i, h, off)
                copy.start()
                sends.append(copy)
    for copy in loads:
        copy.wait()
    lanes = heads * tokens
    for h in range(pieces):
        pair_ready(h, 0)
        for off in range(1, chips):
            for i in range(2):
                to_chip(i, h, off).wait_recv()
        lo, hi = h * lanes, (h + 1) * lanes
        _, numer, denom = weighted(
            [host_acc[:, lo:hi], mine_out[0, h], pair_out[0, h]]
            + [got_out[off, h] for off in range(1, chips)],
            [(host_max[0:1, lo:hi], None), stats_of(mine_stat, 0, h), stats_of(pair_stat, 0, h)]
            + [stats_of(got_stat, off, h) for off in range(1, chips)],
        )
        done = (numer / denom).T
        for j in range(kv):
            block = [done[g * tokens + j * part : g * tokens + (j + 1) * part] for g in range(heads)]
            kv_send[h, j] = jnp.concatenate(block, axis=1).astype(jnp.bfloat16)
        for off in range(1, kv):
            copy = across(h, off, (my_kv + off) % kv, my_kv)
            copy.start()
            sends.append(copy)
        kv_recv[h, my_kv] = kv_send[h, my_kv]
    for h in range(pieces):
        for off in range(1, kv):
            across(h, off, (my_kv + off) % kv, (my_kv + kv - off) % kv).wait_recv()
        for i in range(kv):
            lo = (i * pieces + h) * heads * HD
            result[0, :, lo : lo + heads * HD] = kv_recv[h, i]
    for copy in sends:
        copy.wait_send()


VM = pl.BlockSpec(memory_space=pltpu.VMEM)
ANY = pl.BlockSpec(memory_space=pl.ANY)
SM = pl.BlockSpec(memory_space=pltpu.SMEM)
LIMIT = 62 * 1024 * 1024
MERGE_LIMIT = LIMIT


def body(
    n,
    kv,
    queries,
    suffix_keys,
    suffix_values,
    passage_keys,
    passage_values,
    fresh_keys,
    fresh_values,
    citations,
    selected,
):
    _, tokens, width = queries.shape
    rows = tokens * width // HD
    local, length, _ = passage_keys.shape
    _, cite_count, picks = selected.shape
    chips = n // 2
    bf, f32, i32 = jnp.bfloat16, jnp.float32, jnp.int32
    dma = pltpu.SemaphoreType.DMA
    q_all, cite_all, sel_all, host_acc, host_max = pl.pallas_call(
        functools.partial(gather_kernel, n),
        out_shape=(
            jax.ShapeDtypeStruct((n, tokens, width), bf),
            jax.ShapeDtypeStruct((n, 8, 128), i32),
            jax.ShapeDtypeStruct((n, cite_count, picks), i32),
            jax.ShapeDtypeStruct((HD + ONES, rows), f32),
            jax.ShapeDtypeStruct((8, rows), f32),
        ),
        in_specs=[ANY] * 7,
        out_specs=(ANY, ANY, ANY, VM, VM),
        scratch_shapes=[
            pltpu.VMEM((8, 128), i32),
            pltpu.VMEM(citations.shape, i32),
            pltpu.VMEM(queries.shape, bf),
            pltpu.VMEM(suffix_keys.shape, bf),
            pltpu.VMEM(suffix_values.shape, bf),
            pltpu.VMEM(fresh_keys.shape, bf),
            pltpu.VMEM(fresh_values.shape, bf),
            dma((6,)),
            dma((3,)),
            dma((3, chips)),
            dma((3, chips)),
            dma((3, chips)),
            dma((3, chips)),
        ],
        compiler_params=pltpu.CompilerParams(
            collective_id=0, has_side_effects=True, vmem_limit_bytes=LIMIT
        ),
        name="gather_queries",
    )(queries, suffix_keys, suffix_values, fresh_keys, fresh_values, citations, selected)

    out_all, stat_all = pl.pallas_call(
        slot_kernel,
        out_shape=(
            jax.ShapeDtypeStruct((n, 2, HD, rows // 2), bf),
            jax.ShapeDtypeStruct((n, 2, 8, rows // 2), f32),
        ),
        in_specs=[SM, ANY, ANY, ANY, ANY],
        out_specs=(VM, VM),
        scratch_shapes=[
            pltpu.VMEM((n, tokens, width), bf),
            pltpu.VMEM((n, cite_count, picks), i32),
            pltpu.VMEM(passage_keys.shape, bf),
            pltpu.VMEM(passage_values.shape, bf),
            pltpu.VMEM((local, HD + ONES, length), bf),
            pltpu.VMEM((n, HD + ONES, rows), f32),
            pltpu.VMEM((n, 8, rows), f32),
            pltpu.VMEM((2, 8, rows // 2), f32),
            pltpu.VMEM((length, picks), bf),
            pltpu.VMEM((length, rows // 2), f32),
            pltpu.VMEM((length, rows // 2), f32),
            pltpu.SMEM((n * cite_count + 1,), i32),
            dma((4,)),
        ],
        compiler_params=pltpu.CompilerParams(vmem_limit_bytes=LIMIT),
        name="passage_slots",
    )(cite_all, q_all, sel_all, passage_keys, passage_values)

    return pl.pallas_call(
        functools.partial(merge_kernel, n, kv),
        out_shape=jax.ShapeDtypeStruct((1, tokens // kv, width * kv), bf),
        in_specs=[ANY] * 4,
        out_specs=VM,
        scratch_shapes=[
            pltpu.VMEM((HD + ONES, rows), f32),
            pltpu.VMEM((8, rows), f32),
            *(
                [
                    pltpu.VMEM((chips, 2, HD, rows // 2), bf),
                    pltpu.VMEM((chips, 2, 8, rows // 2), f32),
                ]
                * 4
            ),
            pltpu.VMEM((2, kv, tokens // kv, width // 2), bf),
            pltpu.VMEM((2, kv, tokens // kv, width // 2), bf),
            dma((2,)),
            *([dma((2, 2, chips))] * 5),
            dma((2, kv)),
            dma((2, kv)),
        ],
        compiler_params=pltpu.CompilerParams(
            collective_id=1, has_side_effects=True, vmem_limit_bytes=MERGE_LIMIT
        ),
        name="merge_groups",
    )(out_all, stat_all, host_acc, host_max)


def solution(mesh):
    placed = (
        P("pass", None, "kv"),
        P("pass", None, "kv"),
        P("pass", None, "kv"),
        P("pass", None, "kv"),
        P("pass", None, "kv"),
        P("pass", None, None, "kv"),
        P("pass", None, None, "kv"),
        P("pass", None),
        P("pass", None, None),
    )
    return jax.shard_map(
        functools.partial(body, mesh.shape["pass"], mesh.shape["kv"]),
        mesh=mesh,
        in_specs=placed,
        out_specs=P("pass", "kv", None),
        check_vma=False,
    )
```

profile of v0, /device:TPU:0, one launch (start us, length us, event | category | flops | bytes accessed | tf_op | source)
XLA Modules:
  0.0 47.7 jit_solution(12521265658239445325)
XLA Ops:
  0.0 13.9 %gather_queries.1 = (bf16[8,64,1024]{2,1,0:T(8,128)(2,1)}, s32[8,8,128]{2,1,0:T(8,128)}, s32[8,8,128]{2,1,0:T(8,128)}, f32[144,512]{1,0:T(8,128)}, f32[8,512]{1,0:T(8,128)}) custom-call(bf16[1,64,1024]{2,1,0:T(8,128)(2,1)} %q_ref.1, bf16[1,64,128]{2,1,0:T(8,128)(2,1)} %sk_ref.1, bf16[1,64,128]{2,1,0:T(8,128)(2,1)} %sv_ref.1, ...), custom_call_target="tpu_custom_call" | custom-call | tf_op jit(solution)/shard_map/gather_queries/pallas_call | solution.py:481
  13.9 11.9 %passage_slots.1 = (bf16[8,2,128,256]{3,2,1,0:T(8,128)(2,1)}, f32[8,2,8,256]{3,2,1,0:T(8,128)}) custom-call(s32[8,8,128]{2,1,0:T(8,128)} %get-tuple-element.12.cites, bf16[8,64,1024]{2,1,0:T(8,128)(2,1)} %get-tuple-element.13.q_hbm, s32[8,8,128]{2,1,0:T(8,128)} %get-tuple-element.14.sel_hbm, bf16[4,1024,128]{2,1,0:T(8,128)(2,1)} %k_hbm.1, ...), custom_call_target="tpu_custom_call" | custom-call | tf_op jit(solution)/shard_map/passage_slots/pallas_call | solution.py:513
  25.8 20.3 %merge_groups.1 = bf16[1,16,4096]{2,1,0:T(8,128)(2,1)} custom-call(bf16[8,2,128,256]{3,2,1,0:T(8,128)(2,1)} %get-tuple-element.15.out_all, f32[8,2,8,256]{3,2,1,0:T(8,128)} %get-tuple-element.16.stat_all, f32[144,512]{1,0:T(8,128)} %get-tuple-element.17.host_acc_hbm, f32[8,512]{1,0:T(8,128)} %get-tuple-element.18.host_max_hbm), custom_call_target="tpu_custom_call" | custom-call | tf_op jit(solution)/shard_map/merge_groups/pallas_call | solution.py:540
  46.1 1.6 %copy.11 = bf16[1,16,4096]{2,1,0:T(8,128)(2,1)} copy(bf16[1,16,4096]{2,1,0:T(8,128)(2,1)} %merge_groups.1) | data formatting | bytes 262144
where the time goes:
time: 48.6 us; the launch traced here: 47.7 us
  Pallas kernels  46.1 us (95%)
  local copies, waits for them, and re-layouts  1.57 us (3%)
    pallas_call x1, Pallas kernels, body(): pl.pallas_call(functools.partial(merge_kernel, n, kv), out_shape=jax.Shap...  20.3 us
    pallas_call x1, Pallas kernels, body(): pl.pallas_call(functools.partial(gather_kernel, n), out_shape=(jax.ShapeD...  13.9 us
    pallas_call x1, Pallas kernels, body(): pl.pallas_call(slot_kernel, out_shape=(jax.ShapeDtypeStruct((n, 2, HD, ro...  11.9 us
    unnamed x1, local copies, waits for them, and re-layouts  1.57 us

commit v1 on v0

--- a/solution.py
+++ b/solution.py
@@ -14,6 +14,7 @@
 FACTOR = math.log2(math.e) / math.sqrt(HD)
 ONES = 16
 CHUNK = 256
+KEYS = 256
 
 
 def nt_dot(a, b):
@@ -218,36 +219,50 @@
         picked = sel_all[r, pl.ds(c, 1), :]
         bias[...] = jnp.where(at == picked, very_low, 0.0).astype(jnp.bfloat16)
 
-    def score(r, p, side, place):
-        keys = jnp.concatenate([k_ref[p], bias[...]], axis=1)
+    steps = [slice(lo, lo + KEYS) for lo in range(0, length, KEYS)]
+
+    def score_steps(r, p, side, place):
         cut = heads_half * HD
         q = stack_heads(q_all[r, :, side * cut : (side + 1) * cut], heads_half)
         q = jnp.concatenate([q, jnp.ones((half, picks), jnp.bfloat16)], axis=1)
-        s = nt_dot(keys, q)
-        place[...] = s
-        peak[side] = jnp.broadcast_to(jnp.max(s, axis=0, keepdims=True), (8, half))
-
-    def weigh(r, p, side, place):
+        highest = None
+        for at in steps:
+            keys = jnp.concatenate([k_ref[p, at, :], bias[at, :]], axis=1)
+            s = nt_dot(keys, q)
+            place[at, :] = s
+            here = jnp.max(s.reshape(KEYS // 8, 8, half), axis=0)
+            highest = here if highest is None else jnp.maximum(highest, here)
+            yield
+        peak[side] = jnp.broadcast_to(jnp.max(highest, axis=0, keepdims=True), (8, half))
+
+    def weigh_steps(r, p, side, place):
         lo, hi = side * half, (side + 1) * half
         old = top[r, 0:1, lo:hi]
         new = jnp.maximum(old, peak[side, 0:1, :])
-        w = jnp.exp2((place[...] - new) * FACTOR).astype(jnp.bfloat16)
         scale = jnp.exp2((old - new) * FACTOR)
-        acc[r, :, lo:hi] = acc[r, :, lo:hi] * scale + nn_dot(v_t[p], w)
         top[r, :, lo:hi] = jnp.broadcast_to(new, (8, half))
+        added = acc[r, :, lo:hi] * scale
+        for at in steps:
+            w = jnp.exp2((place[at, :] - new) * FACTOR).astype(jnp.bfloat16)
+            added = added + nn_dot(v_t[p, :, at], w)
+            yield
+        acc[r, :, lo:hi] = added
+
+    def together(*parts):
+        waiting = list(parts)
+        while waiting:
+            waiting = [part for part in waiting if next(part, True) is None]
 
     r, c, p = where(0)
     fill_bias(r, c)
-    score(r, p, 0, first)
+    together(score_steps(r, p, 0, first))
 
     def one_slot(i, carry):
         r, c, p = where(i)
-        score(r, p, 1, second)
-        weigh(r, p, 0, first)
+        together(weigh_steps(r, p, 0, first), score_steps(r, p, 1, second))
         r_next, c_next, p_next = where(i + 1)
         fill_bias(r_next, c_next)
-        score(r_next, p_next, 0, first)
-        weigh(r, p, 1, second)
+        together(weigh_steps(r, p, 1, second), score_steps(r_next, p_next, 0, first))
         return carry
 
     lax.fori_loop(0, count, one_slot, 0)

time: 48.6 us -> 47.1 us (0.969); the launches traced: 47.7 us -> 47.1 us
  Pallas kernels: 46.1 us -> 45.5 us
    pallas_call x1, Pallas kernels: 11.9 us -> 10.3 us  [body(): pl.pallas_call(slot_kernel, out_shape=(jax.ShapeDtypeStruct((n, 2, HD, ro...]
    pallas_call x1, Pallas kernels: 20.3 us -> 21.3 us  [body(): pl.pallas_call(functools.partial(merge_kernel, n, kv), out_shape=jax.Shap...]
where the time goes in v1:
time: 47.1 us
  Pallas kernels  45.5 us (97%)
  local copies, waits for them, and re-layouts  1.57 us (3%)
    pallas_call x1, Pallas kernels, body(): pl.pallas_call(functools.partial(merge_kernel, n, kv), out_shape=jax.Shap...  21.3 us
    pallas_call x1, Pallas kernels, body(): pl.pallas_call(functools.partial(gather_kernel, n), out_shape=(jax.ShapeD...  13.9 us
    pallas_call x1, Pallas kernels, body(): pl.pallas_call(slot_kernel, out_shape=(jax.ShapeDtypeStruct((n, 2, HD, ro...  10.3 us
    unnamed x1, local copies, waits for them, and re-layouts  1.57 us

profile of v1, /device:TPU:0, one launch (start us, length us, event | category | flops | bytes accessed | tf_op | source)
XLA Modules:
  0.0 47.1 jit_solution(7914991344651583514)
XLA Ops:
  0.0 13.9 %gather_queries.1 = (bf16[8,64,1024]{2,1,0:T(8,128)(2,1)}, s32[8,8,128]{2,1,0:T(8,128)}, s32[8,8,128]{2,1,0:T(8,128)}, f32[144,512]{1,0:T(8,128)}, f32[8,512]{1,0:T(8,128)}) custom-call(bf16[1,64,1024]{2,1,0:T(8,128)(2,1)} %q_ref.1, bf16[1,64,128]{2,1,0:T(8,128)(2,1)} %sk_ref.1, bf16[1,64,128]{2,1,0:T(8,128)(2,1)} %sv_ref.1, ...), custom_call_target="tpu_custom_call" | custom-call | tf_op jit(solution)/shard_map/gather_queries/pallas_call | solution.py:496
  13.9 10.3 %passage_slots.1 = (bf16[8,2,128,256]{3,2,1,0:T(8,128)(2,1)}, f32[8,2,8,256]{3,2,1,0:T(8,128)}) custom-call(s32[8,8,128]{2,1,0:T(8,128)} %get-tuple-element.12.cites, bf16[8,64,1024]{2,1,0:T(8,128)(2,1)} %get-tuple-element.13.q_hbm, s32[8,8,128]{2,1,0:T(8,128)} %get-tuple-element.14.sel_hbm, bf16[4,1024,128]{2,1,0:T(8,128)(2,1)} %k_hbm.1, ...), custom_call_target="tpu_custom_call" | custom-call | tf_op jit(solution)/shard_map/passage_slots/pallas_call | solution.py:528
  24.2 21.3 %merge_groups.1 = bf16[1,16,4096]{2,1,0:T(8,128)(2,1)} custom-call(bf16[8,2,128,256]{3,2,1,0:T(8,128)(2,1)} %get-tuple-element.15.out_all, f32[8,2,8,256]{3,2,1,0:T(8,128)} %get-tuple-element.16.stat_all, f32[144,512]{1,0:T(8,128)} %get-tuple-element.17.host_acc_hbm, f32[8,512]{1,0:T(8,128)} %get-tuple-element.18.host_max_hbm), custom_call_target="tpu_custom_call" | custom-call | tf_op jit(solution)/shard_map/merge_groups/pallas_call | solution.py:555
  45.5 1.6 %copy.11 = bf16[1,16,4096]{2,1,0:T(8,128)(2,1)} copy(bf16[1,16,4096]{2,1,0:T(8,128)(2,1)} %merge_groups.1) | data formatting | bytes 262144
